TPU v7x, 256 devices: a whole 4x4x8 slice. The times are simulated.
256 devices in a mesh: expert: 32 (over z, x_hi, core), pipe: 4 (over y), dp: 2 (over x_lo).
Axes of the slice: x: 4 (x_hi: 2, x_lo: 2; x = x_hi * 2 + x_lo), y: 4, z: 8, core: 2. Of those that a mesh axis runs over, the one named last changes fastest.
Arguments:
- tokens: bfloat16 [4096, 3584], P('expert', ('pipe', 'dp')), may hold values from -6 to 6
- routing: int32 [4096, 8], P('expert'), may hold values from 0 to 31, all different within a row; in each aligned block of 128 rows (0 to 127, 128 to 255, ...) at most 48 rows name the same one
- gate_weights: float32 [4096, 8], P('expert'), may hold values from 0.1 to 0.6
- cotangent: bfloat16 [4096, 3584], P('expert', ('pipe', 'dp')), may hold values from -1.5 to 1.5
- w_in: bfloat16 [32, 3584, 2048], P('expert', ('pipe', 'dp')), may hold values from -0.09375 to 0.09375
- w_out: bfloat16 [32, 1024, 3584], P('expert', None, ('pipe', 'dp')), may hold values from -0.1875 to 0.1875
Outputs:
- mixed: bfloat16 [4096, 3584], P('expert', ('pipe', 'dp'))
- tokens_grad: bfloat16 [4096, 3584], P('expert', ('pipe', 'dp'))
- w_in_grad: bfloat16 [32, 3584, 2048], P('expert', ('pipe', 'dp'))
- w_out_grad: bfloat16 [32, 1024, 3584], P('expert', None, ('pipe', 'dp'))
Inputs may be any that keep to these rules, and one draw needn't show every extreme that they name: `routing`: each token names 8 different experts. Among the 128 tokens of one index of the expert axis no expert is named more than 48 times, a bound that some block reaches.
All inputs are finite; a program needn't handle non-finite values.
Results may differ from a plain program's by a relative error of at most 0.029.
Values may be sent and summed in bfloat16 or wider, within the bound.
A program may use at most 128 MiB of HBM per device.

v0:
```python
import jax
import jax.numpy as jnp
from jax import lax
from jax.experimental import pallas as pl
from jax.experimental.pallas import tpu as pltpu
from jax.sharding import PartitionSpec as P

H = 1024
CAP = 48
TOK = 128
W = 448
NZ = 8
NCH = 16
ROWS = 2 * CAP
RY = 64
RX = 32
BW = 384
AHEAD = 3
ORDER = ((0, 0), (2, 0), (-2, 0), (0, 1), (1, 1), (-1, 1), (2, 1), (-2, 1))
ORDER += ((3, 1), (-3, 1), (4, 1), (4, 0), (3, 0), (-3, 0), (1, 0), (-1, 0))
LAST_1 = 10
LOCAL_1 = 3
MESH = pl.DeviceIdType.MESH
F32 = jnp.float32
BF16 = jnp.bfloat16


def nt_dot(a, b):
    return lax.dot_general(a, b, (((1,), (1,)), ((), ())), preferred_element_type=F32)


def tn_dot(a, b):
    return lax.dot_general(a, b, (((0,), (0,)), ((), ())), preferred_element_type=F32)


def dot(a, b):
    return jnp.dot(a, b, preferred_element_type=F32)


def kernel(
    tok_hbm,
    cot_hbm,
    rt_ref,
    gt_ref,
    win_hbm,
    wout_hbm,
    mixed_ref,
    tgrad_ref,
    wig_ref,
    wog_ref,
    tct,
    winp,
    woutp,
    code,
    gate,
    x0,
    xr,
    sb,
    r1,
    r2,
    sx,
    rx,
    g,
    sb2,
    rf,
    q1,
    q2,
    g2,
    outb,
    ret,
    xt,
    acc_in,
    acc_out,
    macc,
    tacc,
    rt2,
    gt2,
    pout,
    pin,
    w_sem,
    ps,
    pr,
    ss,
    rs,
):
    e, p, q = lax.axis_index("expert"), lax.axis_index("pipe"), lax.axis_index("dp")
    z, xhi, core = lax.div(e, 4), lax.rem(lax.div(e, 2), 2), lax.rem(e, 2)
    pu, pd, pf = lax.rem(p + 1, 4), lax.rem(p + 3, 4), lax.rem(p + 2, 4)
    up, dn, xp = (e, pu, q), (e, pd, q), (e, p, 1 - q)
    qo = 1 - q

    def send(src, dst, c, k, dev):
        pltpu.make_async_remote_copy(
            src_ref=src,
            dst_ref=dst,
            send_sem=ss.at[c, k],
            recv_sem=rs.at[c, k],
            device_id=dev,
            device_id_type=MESH,
        ).start()

    def wait(ref, c, k):
        pltpu.make_async_copy(ref, ref, rs.at[c, k]).wait()

    def place(c, sign):
        packed = jnp.int32(0)
        for i, (shift, half) in enumerate(ORDER):
            packed = jnp.where(c == i, 2 * (shift + NZ) + half, packed)
        shift, half = lax.div(packed, 2) - NZ, lax.rem(packed, 2)
        return 2 * lax.rem(z + sign * shift + NZ, NZ) + xhi, half

    barrier = pltpu.get_barrier_semaphore()
    peer = ((2 * z + 1 - xhi) * 2 + core, p, q)

    def greet(dev):
        pl.semaphore_signal(barrier, inc=1, device_id=dev, device_id_type=MESH)

    @pl.loop(0, 16)
    def _(d):
        other = (2 * lax.div(d, 2) + xhi) * 2 + lax.rem(d, 2)

        @pl.when(other != e)
        def _():
            greet((other, p, q))

    for dev in (up, dn, xp, peer):
        greet(dev)

    loads = [
        pltpu.make_async_copy(tok_hbm, tct.at[0, pl.ds(0, W)], w_sem.at[0]),
        pltpu.make_async_copy(cot_hbm, tct.at[0, pl.ds(W, W)], w_sem.at[1]),
        pltpu.make_async_copy(win_hbm, winp.at[pl.ds(0, W)], w_sem.at[2]),
        pltpu.make_async_copy(wout_hbm, woutp.at[pl.ds(64, W)], w_sem.at[3]),
    ]
    for load in loads:
        load.start()
    winp[pl.ds(W, 64), :] = jnp.zeros((64, 2 * H), BF16)
    woutp[pl.ds(0, 64), :] = jnp.zeros((64, H), BF16)

    ids = lax.broadcasted_iota(jnp.int32, (32, TOK), 0)
    before = jnp.where(
        lax.broadcasted_iota(jnp.int32, (TOK, TOK), 0)
        < lax.broadcasted_iota(jnp.int32, (TOK, TOK), 1),
        1.0,
        0.0,
    ).astype(BF16)

    def find_slots(half, rt, gt):
        hit = jnp.zeros((32, TOK), F32)
        weight = jnp.zeros((32, TOK), F32)
        for k in range(8):
            same = rt[k : k + 1, :] == ids
            hit = hit + jnp.where(same, 1.0, 0.0)
            weight = weight + jnp.where(same, gt[k : k + 1, :], 0.0)
        marked = jnp.where(hit > 0.5, dot(hit.astype(BF16), before), -1.0)
        for i in range(16):
            code[half, i, :, :] = marked[2 * i : 2 * i + 2, :]
            gate[half, i, :, :] = weight[2 * i : 2 * i + 2, :]

    find_slots(0, rt_ref, gt_ref)

    row_ids = lax.broadcasted_iota(jnp.int32, (CAP, TOK), 0).astype(F32)
    lanes = lax.broadcasted_iota(jnp.int32, (ROWS, 2 * W), 1)

    def picks(at, half):
        cq, gq = code[half, at], gate[half, at]
        chosen = [cq[j : j + 1, :] == row_ids for j in range(2)]
        pick = [jnp.where(m, 1.0, 0.0) for m in chosen]
        gates = [jnp.where(m, gq[j : j + 1, :], 0.0) for j, m in enumerate(chosen)]
        return jnp.concatenate(pick, axis=0), jnp.concatenate(gates, axis=0)

    def local(c):
        return jnp.logical_or(c == 0, c == LOCAL_1)

    def deliver(src, dst, c, k, at):
        for j in range(2):
            own = jnp.logical_and(local(c), core == j)

            @pl.when(own)
            def _():
                pltpu.make_async_copy(src.at[c, j], dst.at[c, core], rs.at[c, k]).start()

            @pl.when(jnp.logical_not(own))
            def _():
                send(src.at[c, j], dst.at[c, core], c, k, (at * 2 + j, p, q))

    def stage_pick(c):
        at, half = place(c, 1)
        pick, gates = picks(at, half)
        row_gate = jnp.sum(gates, axis=1, keepdims=True)
        rows = nt_dot(pick.astype(BF16), tct[half])
        rows = jnp.where(lanes >= W, rows * row_gate, rows).astype(BF16)
        x0[c] = rows.reshape(2, CAP, 2 * W)
        deliver(x0, xr, c, 0, at)

    def stage_a(c):
        wait(xr.at[c], c, 0)
        rows = xr[c].reshape(ROWS, 2 * W)
        x, dy = rows[:, 0:512], rows[:, 384:896]
        for k, pp in enumerate((pf, pu, pd, p)):
            at = pl.multiple_of(pp * 256, 256)
            gp = dot(x, winp[:, pl.ds(at, 256)]).astype(BF16)
            un = dot(x, winp[:, pl.ds(at + H, 256)]).astype(BF16)
            bk = dot(dy, woutp[:, pl.ds(at, 256)]).astype(BF16)
            for h in range(2):
                s = slice(h * 128, h * 128 + 128)
                for i, v in enumerate((gp, un, bk)):
                    t = slice(i * 128, i * 128 + 128)
                    sb[c, pp, h, :, t] = v[0:RY, s]
                    sb2[c, h, pp, :, t] = v[RY:ROWS, s]
            if k == 0:
                send(sb.at[c, pf, 0], r1.at[c, 0], c, 1, up)
                send(sb.at[c, pf, 1], r1.at[c, 1], c, 2, dn)
            if k == 1:
                send(sb.at[c, pu, 1], r2.at[c, 0], c, 3, up)
            if k == 2:
                send(sb.at[c, pd, 0], r2.at[c, 1], c, 4, dn)
        send(sb2.at[c, qo], rf.at[c], c, 16, xp)

    def by_parity(c, run):
        @pl.when(lax.rem(c, 2) == 0)
        def _():
            run(up, pu, dn, pd)

        @pl.when(lax.rem(c, 2) == 1)
        def _():
            run(dn, pd, up, pu)

    def stage_b(c):
        wait(r1.at[c, 0], c, 1)
        sb[c, pu, 0] = (sb[c, pu, 0].astype(F32) + r1[c, 0].astype(F32)).astype(BF16)
        send(sb.at[c, pu, 0], r2.at[c, 2], c, 5, up)
        wait(r1.at[c, 1], c, 2)
        sb[c, pd, 1] = (sb[c, pd, 1].astype(F32) + r1[c, 1].astype(F32)).astype(BF16)
        send(sb.at[c, pd, 1], r2.at[c, 3], c, 6, dn)
        wait(rf.at[c], c, 16)
        sb2[c, q] = (sb2[c, q].astype(F32) + rf[c].astype(F32)).astype(BF16)

        def run(a, pa, b, pb):
            send(sb2.at[c, q, pf], q1.at[c], c, 17, a)
            send(sb2.at[c, q, pb], q2.at[c, 1], c, 18, b)

        by_parity(c, run)

    def y_sum(c, h):
        return (
            sb[c, p, h].astype(F32)
            + r2[c, 1 - h].astype(F32)
            + r2[c, 2 + h].astype(F32)
        )

    def stage_c(c):
        for k in range(4):
            wait(r2.at[c, k], c, 3 + k)
        sx[c] = y_sum(c, qo).astype(BF16)
        send(sx.at[c], rx.at[c], c, 7, xp)
        wait(q1.at[c], c, 17)

        def run(a, pa, b, pb):
            sb2[c, q, pa] = (sb2[c, q, pa].astype(F32) + q1[c].astype(F32)).astype(BF16)
            send(sb2.at[c, q, pa], q2.at[c, 0], c, 19, a)

        by_parity(c, run)

    def activate(total):
        gp, un, bk = total[:, 0:128], total[:, 128:256], total[:, 256:384]
        s = 1.0 / (1.0 + jnp.exp(-gp))
        act = gp * s
        return jnp.concatenate(
            [act * un, bk * un * (s * (1.0 + gp * (1.0 - s))), bk * act], axis=1
        ).astype(BF16)

    def stage_d(c):
        wait(rx.at[c], c, 7)
        g[c, p, q] = activate(y_sum(c, q) + rx[c].astype(F32))
        mine = g.at[c, p, q]
        send(mine, mine, c, 8, xp)
        send(mine, mine, c, 9, up)
        send(mine, mine, c, 10, dn)
        wait(q2.at[c, 1], c, 18)
        wait(q2.at[c, 0], c, 19)
        g2[c, q, p] = activate(
            sb2[c, q, p].astype(F32) + q2[c, 0].astype(F32) + q2[c, 1].astype(F32)
        )
        mine2 = g2.at[c, q, p]
        send(mine2, mine2, c, 20, up)
        send(mine2, mine2, c, 21, dn)

    def stage_e(c):
        other = g.at[c, p, qo]
        wait(other, c, 8)
        send(other, other, c, 11, up)
        send(other, other, c, 12, dn)
        wait(g2.at[c, q, pd], c, 20)
        wait(g2.at[c, q, pu], c, 21)

        def run(a, pa, b, pb):
            send(g2.at[c, q, pb], g2.at[c, q, pb], c, 22, a)

        by_parity(c, run)

    def stage_f(c):
        wait(g.at[c, pd, q], c, 9)
        wait(g.at[c, pu, q], c, 10)
        wait(g.at[c, pd, qo], c, 11)
        wait(g.at[c, pu, qo], c, 12)
        send(g.at[c, pd, 0], g.at[c, pd, 0], c, 13, up)
        send(g.at[c, pu, 1], g.at[c, pu, 1], c, 14, dn)
        wait(g2.at[c, q, pf], c, 22)
        send(g2.at[c, q], g2.at[c, q], c, 23, xp)

    def stage_g(c):
        wait(g.at[c, pf, 0], c, 13)
        wait(g.at[c, pf, 1], c, 14)
        wait(g2.at[c, qo], c, 23)

        def part(k):
            s = slice(k * 128, k * 128 + 128)
            y = [g[c, i // 2, i % 2, :, s] for i in range(8)]
            x = [g2[c, i % 2, i // 2, :, s] for i in range(8)]
            return jnp.concatenate(
                [jnp.concatenate(y, axis=1), jnp.concatenate(x, axis=1)], axis=0
            )

        back = nt_dot(part(1), winp[:, 0:H]) + nt_dot(part(2), winp[:, H : 2 * H])
        out = nt_dot(part(0), woutp[...])
        for j in range(2):
            s = slice(j * CAP, j * CAP + CAP)
            outb[c, j, :, 0:384] = back[s, 0:384].astype(BF16)
            outb[c, j, :, 384:512] = (back[s, 384:512] + out[s, 0:128]).astype(BF16)
            outb[c, j, :, 512:896] = out[s, 128:512].astype(BF16)
        deliver(outb, ret, c, 15, place(c, -1)[0])

    def stage_h(c):
        xt[...] = xr[c].reshape(ROWS, 2 * W).T

        @pl.loop(0, 4)
        def _(pp):
            def pair(k):
                s = slice(k * 128, k * 128 + 128)
                y = [g[c, pp, h, :, s] for h in range(2)]
                x = [g2[c, h, pp, :, s] for h in range(2)]
                return jnp.concatenate(
                    [jnp.concatenate(y, axis=1), jnp.concatenate(x, axis=1)], axis=0
                )

            at = pl.multiple_of(pp * 256, 256)
            acc_in[:, pl.ds(at, 256)] += dot(xt[0:512, :], pair(1))
            acc_in[:, pl.ds(at + H, 256)] += dot(xt[0:512, :], pair(2))
            acc_out[:, pl.ds(at, 256)] += dot(xt[384:896, :], pair(0))

    def combine(c):
        wait(ret.at[c], c, 15)
        at, half = place(c, 1)
        pick, gates = picks(at, half)
        rows = ret[c].reshape(ROWS, 2 * W)
        high = gates.astype(BF16)
        low = (gates - high.astype(F32)).astype(BF16)
        tacc[half] += tn_dot(rows[:, 0:512], pick.astype(BF16))
        macc[half] += tn_dot(rows[:, 384:896], high) + tn_dot(rows[:, 384:896], low)

    loads[0].wait()
    loads[1].wait()
    pl.semaphore_wait(barrier, 19)

    def to_peer(src, dst, k):
        pltpu.make_async_remote_copy(
            src_ref=src,
            dst_ref=dst,
            send_sem=ps.at[k],
            recv_sem=pr.at[k],
            device_id=peer,
            device_id_type=MESH,
        ).start()

    def peer_wait(ref, sem):
        pltpu.make_async_copy(ref, ref, sem).wait()

    to_peer(rt_ref, rt2, 0)
    to_peer(gt_ref, gt2, 1)
    to_peer(tct.at[0], tct.at[1], 2)

    @pl.loop(0, AHEAD)
    def _(c):
        stage_pick(c)

    acc_in[...] = jnp.zeros_like(acc_in)
    acc_out[...] = jnp.zeros_like(acc_out)
    macc[...] = jnp.zeros_like(macc)
    tacc[...] = jnp.zeros_like(tacc)
    loads[2].wait()
    loads[3].wait()

    stages = (
        (stage_f, 5),
        (stage_e, 4),
        (stage_d, 3),
        (stage_c, 2),
        (stage_b, 1),
        (stage_a, 0),
        (stage_g, 6),
        (stage_h, 6),
        (combine, 8),
    )

    def guarded(stage, c):
        @pl.when(jnp.logical_and(c >= 0, c < NCH))
        def _():
            stage(c)

    @pl.loop(0, NCH + 6)
    def _(s):
        for stage, lag in stages:
            guarded(stage, s - lag)
            if lag == 0:

                @pl.when(s == 0)
                def _():
                    peer_wait(rt2, pr.at[0])
                    peer_wait(gt2, pr.at[1])
                    find_slots(1, rt2, gt2)
                    peer_wait(tct.at[1], pr.at[2])

                for k in range(2):
                    guarded(stage_pick, AHEAD + 2 * s + k)

        @pl.when(s == LAST_1 + 8)
        def _():
            pout[0:W, :] = tacc[1, 0:W, :].astype(BF16)
            pout[W : 2 * W, :] = macc[1, 64:512, :].astype(BF16)
            to_peer(pout, pin, 3)

    wig_ref[...] = acc_in[0:W, :].astype(BF16)
    wog_ref[...] = acc_out[64:512, :].astype(BF16)
    peer_wait(pin, pr.at[3])

    @pl.loop(NCH - 2, NCH)
    def _(c):
        combine(c)

    tgrad_ref[...] = (tacc[0, 0:W, :] + pin[0:W, :].astype(F32)).astype(BF16)
    mixed_ref[...] = (macc[0, 64:512, :] + pin[W : 2 * W, :].astype(F32)).astype(BF16)
    peer_wait(rt2, ps.at[0])
    peer_wait(gt2, ps.at[1])
    peer_wait(pin, ps.at[2])
    peer_wait(pin, ps.at[3])

    def sent(ref, c, k):
        pltpu.make_async_copy(ref, ref, ss.at[c, k]).wait()

    @pl.loop(0, NCH)
    def _(c):
        @pl.when(local(c))
        def _():
            sent(x0.at[c, 0], c, 0)
            sent(outb.at[c, 0], c, 15)

        @pl.when(jnp.logical_not(local(c)))
        def _():
            sent(x0.at[c], c, 0)
            sent(outb.at[c], c, 15)

        for k in range(1, 15):
            sent(sx.at[c], c, k)
        for k in (16, 23):
            sent(rf.at[c], c, k)
        for k in range(17, 23):
            sent(q1.at[c], c, k)


def shards(tokens, routing, gate_weights, cotangent, w_in, w_out):
    vmem = pl.BlockSpec(memory_space=pltpu.VMEM)
    hbm = pl.BlockSpec(memory_space=pl.ANY)
    dma = pltpu.SemaphoreType.DMA
    mixed, tgrad, wig, wog = pl.pallas_call(
        kernel,
        name="experts",
        out_shape=(
            jax.ShapeDtypeStruct((W, TOK), BF16),
            jax.ShapeDtypeStruct((W, TOK), BF16),
            jax.ShapeDtypeStruct((W, 2 * H), BF16),
            jax.ShapeDtypeStruct((W, H), BF16),
        ),
        in_specs=[hbm, hbm, vmem, vmem, hbm, hbm],
        out_specs=(vmem, vmem, vmem, vmem),
        scratch_shapes=[
            pltpu.VMEM((2, 2 * W, TOK), BF16),
            pltpu.VMEM((512, 2 * H), BF16),
            pltpu.VMEM((512, H), BF16),
            pltpu.VMEM((2, 16, 2, TOK), F32),
            pltpu.VMEM((2, 16, 2, TOK), F32),
            pltpu.VMEM((NCH, 2, CAP, 2 * W), BF16),
            pltpu.VMEM((NCH, 2, CAP, 2 * W), BF16),
            pltpu.VMEM((NCH, 4, 2, RY, BW), BF16),
            pltpu.VMEM((NCH, 2, RY, BW), BF16),
            pltpu.VMEM((NCH, 4, RY, BW), BF16),
            pltpu.VMEM((NCH, RY, BW), BF16),
            pltpu.VMEM((NCH, RY, BW), BF16),
            pltpu.VMEM((NCH, 4, 2, RY, BW), BF16),
            pltpu.VMEM((NCH, 2, 4, RX, BW), BF16),
            pltpu.VMEM((NCH, 4, RX, BW), BF16),
            pltpu.VMEM((NCH, RX, BW), BF16),
            pltpu.VMEM((NCH, 2, RX, BW), BF16),
            pltpu.VMEM((NCH, 2, 4, RX, BW), BF16),
            pltpu.VMEM((NCH, 2, CAP, 2 * W), BF16),
            pltpu.VMEM((NCH, 2, CAP, 2 * W), BF16),
            pltpu.VMEM((2 * W, ROWS), BF16),
            pltpu.VMEM((512, 2 * H), F32),
            pltpu.VMEM((512, H), F32),
            pltpu.VMEM((2, 512, TOK), F32),
            pltpu.VMEM((2, 512, TOK), F32),
            pltpu.VMEM((8, TOK), jnp.int32),
            pltpu.VMEM((8, TOK), F32),
            pltpu.VMEM((2 * W, TOK), BF16),
            pltpu.VMEM((2 * W, TOK), BF16),
            dma((4,)),
            dma((4,)),
            dma((4,)),
            dma((NCH, 24)),
            dma((NCH, 24)),
        ],
        compiler_params=pltpu.CompilerParams(
            collective_id=0, has_side_effects=True, vmem_limit_bytes=62 << 20
        ),
    )(tokens.T, cotangent.T, routing.T, gate_weights.T, w_in[0], w_out[0].T)
    return mixed.T, tgrad.T, wig[None], wog.T[None]


def solution(mesh):
    placed = (
        P("expert", ("pipe", "dp")),
        P("expert", None),
        P("expert", None),
        P("expert", ("pipe", "dp")),
        P("expert", ("pipe", "dp"), None),
        P("expert", None, ("pipe", "dp")),
    )
    return jax.shard_map(
        shards,
        mesh=mesh,
        in_specs=placed,
        out_specs=(
            P("expert", ("pipe", "dp")),
            P("expert", ("pipe", "dp")),
            P("expert", ("pipe", "dp"), None),
            P("expert", None, ("pipe", "dp")),
        ),
        check_vma=False,
    )
```

profile of v0, /device:TPU:3, one launch (start us, length us, event | category | flops | bytes accessed | tf_op | source)
XLA Modules:
  0.0 190.1 jit_solution(13232496198894271005)
XLA Ops:
  0.6 182.5 %experts.1 = (bf16[448,128]{1,0:T(8,128)(2,1)}, bf16[448,128]{1,0:T(8,128)(2,1)}, bf16[448,2048]{1,0:T(8,128)(2,1)}, bf16[448,1024]{1,0:T(8,128)(2,1)}) custom-call(bf16[448,128]{1,0:T(8,128)(2,1)} %bitcast.20, bf16[448,128]{1,0:T(8,128)(2,1)} %bitcast.21, s32[8,128]{1,0:T(8,128)} %bitcast.22, f32[8,128]{1,0:T(8,128)} %bitcast.23, ...), custom_call_target="tpu_custom_call" | custom-call | tf_op jit(solution)/shard_map/experts/pallas_call | solution.py:475
  183.1 1.6 copy.14
  184.6 1.6 copy.15
  186.2 0.0 copy-start
  186.2 3.0 %copy.16 = bf16[1,448,2048]{2,1,0:T(8,128)(2,1)} copy(bf16[1,448,2048]{2,1,0:T(8,128)(2,1)} %bitcast.14) | data formatting | bytes 3670016
  189.2 0.0 copy-done
  189.2 0.9 copy.17
Async XLA Ops:
  186.2 3.0 %copy-start = (bf16[448,1024]{1,0:T(8,128)(2,1)S(1)}, bf16[448,1024]{1,0:T(8,128)(2,1)}, u32[]{:S(2)}) copy-start(bf16[448,1024]{1,0:T(8,128)(2,1)} %get-tuple-element.11) | copy-start | bytes 2752516
where the time goes:
time: 190 us
  Pallas kernels  182 us (96%)
  local copies, waits for them, and re-layouts  7.05 us (4%)
    pallas_call x1, Pallas kernels, shards(): pl.pallas_call(kernel, name='experts', out_shape=(jax.ShapeDtypeStruct((W...  182 us
    unnamed x6, local copies, waits for them, and re-layouts  7.05 us

commit v1 on v0

--- a/solution.py
+++ b/solution.py
@@ -16,9 +16,11 @@
 RX = 32
 BW = 384
 AHEAD = 3
-ORDER = ((0, 0), (2, 0), (-2, 0), (0, 1), (1, 1), (-1, 1), (2, 1), (-2, 1))
-ORDER += ((3, 1), (-3, 1), (4, 1), (4, 0), (3, 0), (-3, 0), (1, 0), (-1, 0))
-LAST_1 = 10
+BATCH = 4
+LAG = 7
+ORDER = ((0, 0), (1, 0), (2, 0), (0, 1), (-1, 1), (3, 1), (-3, 1), (4, 1))
+ORDER += ((4, 0), (3, 0), (-3, 0), (2, 1), (-2, 1), (1, 1), (-2, 0), (-1, 0))
+LAST_1 = 13
 LOCAL_1 = 3
 MESH = pl.DeviceIdType.MESH
 F32 = jnp.float32
@@ -331,18 +333,21 @@
             outb[c, j, :, 512:896] = out[s, 128:512].astype(BF16)
         deliver(outb, ret, c, 15, place(c, -1)[0])
 
-    def stage_h(c):
-        xt[...] = xr[c].reshape(ROWS, 2 * W).T
+    def stage_h(first):
+        rows = xr[pl.ds(first, BATCH)].reshape(BATCH * ROWS, 2 * W)
+        xt[...] = rows.T
 
         @pl.loop(0, 4)
         def _(pp):
             def pair(k):
                 s = slice(k * 128, k * 128 + 128)
-                y = [g[c, pp, h, :, s] for h in range(2)]
-                x = [g2[c, h, pp, :, s] for h in range(2)]
-                return jnp.concatenate(
-                    [jnp.concatenate(y, axis=1), jnp.concatenate(x, axis=1)], axis=0
-                )
+                parts = []
+                for b in range(BATCH):
+                    c = first + b
+                    y = [g[c, pp, h, :, s] for h in range(2)]
+                    x = [g2[c, h, pp, :, s] for h in range(2)]
+                    parts += [jnp.concatenate(y, axis=1), jnp.concatenate(x, axis=1)]
+                return jnp.concatenate(parts, axis=0)
 
             at = pl.multiple_of(pp * 256, 256)
             acc_in[:, pl.ds(at, 256)] += dot(xt[0:512, :], pair(1))
@@ -399,8 +404,7 @@
         (stage_b, 1),
         (stage_a, 0),
         (stage_g, 6),
-        (stage_h, 6),
-        (combine, 8),
+        (combine, LAG),
     )
 
     def guarded(stage, c):
@@ -414,7 +418,7 @@
             guarded(stage, s - lag)
             if lag == 0:
 
-                @pl.when(s == 0)
+                @pl.when(s == 1)
                 def _():
                     peer_wait(rt2, pr.at[0])
                     peer_wait(gt2, pr.at[1])
@@ -422,19 +426,31 @@
                     peer_wait(tct.at[1], pr.at[2])
 
                 for k in range(2):
-                    guarded(stage_pick, AHEAD + 2 * s + k)
-
-        @pl.when(s == LAST_1 + 8)
+                    pick_at = AHEAD + 2 * (s - 1) + k
+                    guarded(stage_pick, jnp.where(s > 0, pick_at, NCH))
+
+        done = s - 5
+
+        @pl.when(
+            jnp.logical_and(
+                jnp.logical_and(done >= BATCH, done < NCH), lax.rem(done, BATCH) == 0
+            )
+        )
+        def _():
+            stage_h(done - BATCH)
+
+        @pl.when(s == LAST_1 + LAG)
         def _():
             pout[0:W, :] = tacc[1, 0:W, :].astype(BF16)
             pout[W : 2 * W, :] = macc[1, 64:512, :].astype(BF16)
             to_peer(pout, pin, 3)
 
+    stage_h(NCH - BATCH)
     wig_ref[...] = acc_in[0:W, :].astype(BF16)
     wog_ref[...] = acc_out[64:512, :].astype(BF16)
     peer_wait(pin, pr.at[3])
 
-    @pl.loop(NCH - 2, NCH)
+    @pl.loop(NCH + 6 - LAG, NCH)
     def _(c):
         combine(c)
 
@@ -504,7 +520,7 @@
             pltpu.VMEM((NCH, 2, 4, RX, BW), BF16),
             pltpu.VMEM((NCH, 2, CAP, 2 * W), BF16),
             pltpu.VMEM((NCH, 2, CAP, 2 * W), BF16),
-            pltpu.VMEM((2 * W, ROWS), BF16),
+            pltpu.VMEM((2 * W, BATCH * ROWS), BF16),
             pltpu.VMEM((512, 2 * H), F32),
             pltpu.VMEM((512, H), F32),
             pltpu.VMEM((2, 512, TOK), F32),

time: 190 us -> 215 us (1.13)
  the two profiles are of different devices: /device:TPU:3 before, /device:TPU:1 now
where the time goes in v1:
time: 215 us; the launch traced here: 214 us
  Pallas kernels  207 us (96%)
  local copies, waits for them, and re-layouts  7.05 us (3%)
    pallas_call x1, Pallas kernels, shards(): pl.pallas_call(kernel, name='experts', out_shape=(jax.ShapeDtypeStruct((W...  207 us
    unnamed x6, local copies, waits for them, and re-layouts  7.05 us

profile of v1, /device:TPU:1, one launch (start us, length us, event | category | flops | bytes accessed | tf_op | source)
XLA Modules:
  0.0 214.4 jit_solution(10702310058934020434)
XLA Ops:
  0.6 206.7 %experts.1 = (bf16[448,128]{1,0:T(8,128)(2,1)}, bf16[448,128]{1,0:T(8,128)(2,1)}, bf16[448,2048]{1,0:T(8,128)(2,1)}, bf16[448,1024]{1,0:T(8,128)(2,1)}) custom-call(bf16[448,128]{1,0:T(8,128)(2,1)} %bitcast.20, bf16[448,128]{1,0:T(8,128)(2,1)} %bitcast.21, s32[8,128]{1,0:T(8,128)} %bitcast.22, f32[8,128]{1,0:T(8,128)} %bitcast.23, ...), custom_call_target="tpu_custom_call" | custom-call | tf_op jit(solution)/shard_map/experts/pallas_call | solution.py:491
  207.3 1.6 copy.14
  208.9 1.6 copy.15
  210.4 0.0 copy-start
  210.4 3.0 %copy.16 = bf16[1,448,2048]{2,1,0:T(8,128)(2,1)} copy(bf16[1,448,2048]{2,1,0:T(8,128)(2,1)} %bitcast.14) | data formatting | bytes 3670016
  213.5 0.0 copy-done
  213.5 0.9 copy.17
Async XLA Ops:
  210.4 3.0 %copy-start = (bf16[448,1024]{1,0:T(8,128)(2,1)S(1)}, bf16[448,1024]{1,0:T(8,128)(2,1)}, u32[]{:S(2)}) copy-start(bf16[448,1024]{1,0:T(8,128)(2,1)} %get-tuple-element.11) | copy-start | bytes 2752516
